TPU v7x, 32 devices: a whole 2x2x4 slice. The times are simulated.
32 devices in a mesh: groups: 2 (over y), fsdp: 4 (over z), dp: 2 (over x), pair: 2 (over core).
Axes of the slice: x: 2, y: 2, z: 4, core: 2. Of those that a mesh axis runs over, the one named last changes fastest.
Arguments:
- hidden_input: bfloat16 [4096, 8192], P(('groups', 'fsdp', 'dp', 'pair')), parts along dimension 0, may hold values from -6 to 6
- norm_gain_vector: float32 [8192], replicated, may hold values from 0.5 to 18, as said below
- value_matrix: bfloat16 [8192, 768], P('fsdp'), may hold values from -0.0625 to 0.0625
- adapter_down_map: bfloat16 [16384, 64], P(('groups', 'fsdp')), parts along dimension 0, may hold values from -0.0625 to 0.0625
- adapter_up_map: bfloat16 [128, 768], P('groups'), parts along dimension 0, may hold values from -5 to 5
- values_gradient: bfloat16 [4096, 768], P(('groups', 'fsdp', 'dp', 'pair')), parts along dimension 0, may hold values from -6 to 6
Outputs:
- grad_hidden: bfloat16 [4096, 8192], P(('groups', 'fsdp', 'dp', 'pair')), parts along dimension 0
- grad_down: float32 [16384, 64], P(('groups', 'fsdp')), parts along dimension 0
- grad_up: float32 [128, 768], P('groups'), parts along dimension 0
There are 2 independent parts, one for each index of `groups`. A program takes and returns all parts, laid end to end along the dimension named above; an argument that names none is the same for every part. Nothing has to cross between parts.
Inputs may be any that keep to these rules, and one draw needn't show every extreme that they name: `norm_gain_vector`: positive gains.
All inputs are finite; a program needn't handle non-finite values.
Results may differ from a plain program's by a relative error of at most 0.0085.
Values may be sent and summed in bfloat16 or wider, within the bound.
A program may use at most 64 MiB of HBM per device.

v0:
```python
import math

import jax
import jax.numpy as jnp
from jax import lax
from jax.sharding import PartitionSpec as P

MODEL_WIDTH = 8192
ADAPTER_RANK = 64


norm_eps = 1e-05
adapter_scale = 2.0


def contract_last(left, right):
    return lax.dot_general(
        left, right, (((1,), (1,)), ((), ())), preferred_element_type=jnp.float32
    )


def contract_leading(left, right):
    return lax.dot_general(
        left, right, (((0,), (0,)), ((), ())), preferred_element_type=jnp.float32
    )


def local(
    hidden_input, norm_gain_vector, value_matrix, adapter_down_map, adapter_up_map, values_gradient
):
    width = hidden_input.shape[1]
    stream = hidden_input.astype(jnp.float32)
    inv_rms = lax.rsqrt(jnp.mean(stream * stream, axis=1, keepdims=True) + norm_eps)
    normalized_input = (stream * inv_rms * norm_gain_vector).astype(jnp.bfloat16)
    upward_product = (
        adapter_scale
        * jnp.dot(values_gradient, adapter_up_map.T, preferred_element_type=jnp.float32)
    ).astype(jnp.bfloat16)
    every_values, every_upward = (
        lax.all_gather(values_gradient, "fsdp", axis=0, tiled=True),
        lax.all_gather(upward_product, "fsdp", axis=0, tiled=True),
    )
    columns = contract_last(every_values, value_matrix) + contract_last(
        every_upward, adapter_down_map
    )
    gradient_normalized = lax.all_to_all(
        columns.astype(jnp.bfloat16), "fsdp", split_axis=0, concat_axis=1, tiled=True
    )
    window = normalized_input
    latent_f = jnp.dot(
        window,
        lax.all_gather(adapter_down_map, "fsdp", axis=0, tiled=True),
        preferred_element_type=jnp.float32,
    )
    scaled = gradient_normalized.astype(jnp.float32) * norm_gain_vector
    grad_stream = inv_rms * scaled - stream * (inv_rms**3 / width) * jnp.sum(
        scaled * stream, axis=1, keepdims=True
    )
    latent_code = latent_f.astype(jnp.bfloat16)
    window = normalized_input
    down_shard = lax.psum_scatter(
        contract_leading(window, upward_product), "fsdp", scatter_dimension=0, tiled=True
    )
    up_portion = adapter_scale * contract_leading(latent_code, values_gradient)
    down_shard = lax.psum(down_shard, ("dp", "pair"))
    up_full = lax.psum(up_portion, ("fsdp", "dp", "pair"))
    total = lax.psum(jnp.sum(down_shard * down_shard), "fsdp") + jnp.sum(up_full * up_full)
    factor = jnp.minimum(1.0, 0.5 * math.sqrt(MODEL_WIDTH * ADAPTER_RANK) / jnp.sqrt(total))
    return (grad_stream.astype(jnp.bfloat16), factor * down_shard, factor * up_full)


def solution(mesh):
    return jax.shard_map(
        local,
        mesh=mesh,
        in_specs=(
            P(("groups", "fsdp", "dp", "pair"), None),
            P(),
            P("fsdp", None),
            P(("groups", "fsdp"), None),
            P("groups", None),
            P(("groups", "fsdp", "dp", "pair"), None),
        ),
        out_specs=(
            P(("groups", "fsdp", "dp", "pair"), None),
            P(("groups", "fsdp"), None),
            P("groups", None),
        ),
        check_vma=False,
    )
```

profile of v0, /device:TPU:0, one launch (start us, length us, event | category | flops | bytes accessed | tf_op | source)
XLA Modules:
  0.0 322.7 jit_solution(588120099054937987)
XLA Ops:
  7.2 0.0 copy-start
  7.2 0.0 reduce-scatter.2.cloned.1.call-start
  7.2 21.6 %all_gather.9 = bf16[512,768]{1,0:T(8,128)(2,1)S(1)} all-gather(bf16[128,768]{1,0:T(8,128)(2,1)} %param.11), channel_id=1, replica_groups=mesh['groups'=2,'fsdp'=4,'dp'=2,'pair'=2] {'fsdp'}, dimensions={0}, use_global_device_ids=true | all-gather | bytes 983040 | tf_op jit(solution)/shard_map/all_gather | solution.py:40
  28.9 1.2 fusion.7
  30.1 12.0 %all_gather.10 = bf16[512,64]{0,1:T(8,128)(2,1)S(1)} all-gather(bf16[128,64]{0,1:T(8,128)(2,1)S(1)} %fusion.7), channel_id=1, replica_groups=mesh['groups'=2,'fsdp'=4,'dp'=2,'pair'=2] {'fsdp'}, dimensions={0}, use_global_device_ids=true | all-gather | bytes 81920 | tf_op jit(solution)/shard_map/all_gather | solution.py:41
  42.0 0.0 copy-done
  42.1 0.0 copy-start.3
  42.1 1.8 fusion.13
  43.9 0.0 copy-done.3
  43.9 0.7 add_convert_fusion
  44.6 46.4 %all_to_all.13 = bf16[4,128,2048]{2,1,0:T(8,128)(2,1)S(1)} all-to-all(bf16[4,128,2048]{2,1,0:T(8,128)(2,1)S(1)} %bitcast.16), channel_id=1, replica_groups=mesh['groups'=2,'fsdp'=4,'dp'=2,'pair'=2] {'fsdp'}, dimensions={0} | all-to-all | bytes 4194304 | tf_op jit(solution)/shard_map/all_to_all | solution.py:46
  91.1 0.5 convert_bitcast_fusion
  91.6 0.0 copy-start.2
  91.6 0.0 copy-start.5
  91.6 0.5 copy.10
  92.1 0.0 copy-start.1
  92.1 1.9 copy-done.1
  94.0 0.0 copy-done.2
  94.0 0.0 copy-done.5
  94.0 1.2 fusion
  95.2 0.0 copy-start.4
  95.2 2.2 fusion.10
  97.4 0.0 reduce-scatter.2.cloned.1.call-update
  97.4 0.0 all-gather.2.cloned.1.call-start
  97.5 0.7 all-gather.2.cloned.1.call-update
  98.2 0.0 all-reduce.3.cloned.1.call-start
  98.2 42.3 %reduce-scatter.2.cloned.1.call-done = f32[2048,64]{0,1:T(8,128)} async-done(((f32[8192,64]{0,1:T(8,128)}), f32[2048,64]{0,1:T(8,128)}) %reduce-scatter.2.cloned.1.call-update) | async-done | bytes 524304 | tf_op jit(solution)/shard_map/reduce_scatter | solution.py:61
  140.5 0.0 all-reduce.3.cloned.1.call-update
  140.6 0.0 all-reduce.5.cloned.1.call-start
  140.6 28.9 %all-gather.2.cloned.1.call-done = bf16[8192,64]{0,1:T(8,128)(2,1)} async-done(((bf16[2048,64]{0,1:T(8,128)(2,1)}), bf16[8192,64]{0,1:T(8,128)(2,1)}) %all-gather.2.cloned.1.call-update) | async-done | bytes 1048592 | tf_op jit(solution)/shard_map/all_gather | solution.py:52
  169.5 0.0 copy-done.4
  169.5 3.5 %convolution_multiply_fusion = f32[64,768]{1,0:T(8,128)} fusion(bf16[128,768]{1,0:T(8,128)(2,1)S(1)} %copy-done.4, bf16[8192,64]{0,1:T(8,128)(2,1)} %all-gather.2.cloned.1.call-done, bf16[128,8192]{1,0:T(8,128)(2,1)} %param.6, f32[8192]{0:T(1024)S(1)} %copy-done.5, f32[128]{0:T(128)S(1)} %get-tuple-element.5), kind=kOutput, calls=%fused_computation.13 | convolution fusion | flops 151052288 | bytes 3572224 | tf_op jit(solution)/shard_map/dot_general | solution.py:23
  173.0 0.0 all-reduce.5.cloned.1.call-update
  173.1 5.3 %fusion.3 = bf16[128,8192]{1,0:T(8,128)(2,1)} fusion(bf16[128,8192]{1,0:T(8,128)(2,1)} %param.6, f32[128,8192]{1,0:T(8,128)} %bitcast.15, f32[128]{0:T(128)S(1)} %get-tuple-element.4, f32[128]{0:T(128)S(1)} %get-tuple-element.6, f32[8192]{0:T(1024)S(1)} %copy-done.5, f32[128]{0:T(128)S(1)} %get-tuple-element.5), kind=kLoop, calls=%fused_computation.7 | loop fusion | flops 7340032 | bytes 8422912 | tf_op jit(solution)/shard_map/convert_element_type | solution.py:69
  178.4 26.3 %all-reduce.3.cloned.1.call-done = f32[2048,64]{0,1:T(8,128)} async-done(((f32[2048,64]{0,1:T(8,128)}), f32[2048,64]{0,1:T(8,128)}) %all-reduce.3.cloned.1.call-update) | async-done | bytes 524304 | tf_op jit(solution)/shard_map/psum | solution.py:65
  204.7 1.8 multiply_reduce_fusion
  206.5 92.0 %all-reduce.5.cloned.1.call-done = f32[64,768]{1,0:T(8,128)} async-done(((f32[64,768]{1,0:T(8,128)}), f32[64,768]{1,0:T(8,128)}) %all-reduce.5.cloned.1.call-update) | async-done | bytes 196624 | tf_op jit(solution)/shard_map/psum | solution.py:66
  298.5 1.6 multiply_reduce_fusion.1
  300.1 11.2 %psum.22 = f32[]{:T(128)} all-reduce(f32[]{:T(128)} %multiply_reduce_fusion), channel_id=1, replica_groups=mesh['groups'=2,'fsdp'=4,'dp'=2,'pair'=2] {'fsdp'}, use_global_device_ids=true, to_apply=%region_5.0 | all-reduce | flops 1 | bytes 8 | tf_op jit(solution)/shard_map/psum | solution.py:67
  312.7 1.9 broadcast_multiply_fusion
  314.6 1.6 broadcast_multiply_fusion.1
  (1 shorter events, 0.0 us)
Async XLA Ops:
  7.2 34.9 %copy-start = (bf16[2048,768]{1,0:T(8,128)(2,1)S(1)}, bf16[2048,768]{1,0:T(8,128)(2,1)}, u32[]{:S(2)}) copy-start(bf16[2048,768]{1,0:T(8,128)(2,1)} %param.8) | copy-start | bytes 9437188
  7.2 133.4 %reduce-scatter.2.cloned.1.call-start = ((), (), s32[]{:S(2)}) async-start(), calls=%async_computation.2 | async-start | bytes 2621440 | tf_op jit(solution)/shard_map/reduce_scatter | solution.py:61
  42.1 1.8 copy-start.3
  91.6 2.5 copy-start.2
  91.6 2.4 copy-start.5
  92.1 1.9 copy-start.1
  95.2 74.3 %copy-start.4 = (bf16[128,768]{1,0:T(8,128)(2,1)S(1)}, bf16[128,768]{1,0:T(8,128)(2,1)}, u32[]{:S(2)}) copy-start(bf16[128,768]{1,0:T(8,128)(2,1)} %param.11) | copy-start | bytes 589828
  97.4 72.1 %all-gather.2.cloned.1.call-start = ((), (), s32[]{:S(2)}) async-start(), calls=%async_computation.4 | async-start | bytes 1310720 | tf_op jit(solution)/shard_map/all_gather | solution.py:52
  98.2 106.5 %all-reduce.3.cloned.1.call-start = ((), (), s32[]{:S(2)}) async-start(), calls=%async_computation.3 | async-start | bytes 1048576 | tf_op jit(solution)/shard_map/psum | solution.py:65
  140.6 157.9 %all-reduce.5.cloned.1.call-start = ((), (), s32[]{:S(2)}) async-start(), calls=%async_computation.5 | async-start | bytes 393216 | tf_op jit(solution)/shard_map/psum | solution.py:66
Sparse Core Ops, SparseCore 0:
  97.6 42.9 reduce-scatter.1
  142.2 27.2 all-gather.1
  172.0 32.6 all-reduce.2
  208.9 89.5 all-reduce.4
where the time goes:
time: 323 us
  waiting for transfers between devices  190 us (59%)
  blocking collectives  91.3 us (28%)
  between operations  15.2 us (5%)
  other arithmetic  13.9 us (4%)
  matrix products  9.43 us (3%)
    psum x1, waiting for transfers between devices, local(): up_full = lax.psum(up_portion, ('fsdp', 'dp', 'pair'))  92 us
    all_to_all x1, blocking collectives, local(): lax.all_to_all(columns.astype(jnp.bfloat16), 'fsdp', split_axis=0, concat...  46.4 us
    reduce_scatter x1, waiting for transfers between devices, local(): lax.psum_scatter(contract_leading(window, upward_product), 'fsdp', scatte...  42.3 us
    all_gather x1, waiting for transfers between devices, local(): lax.all_gather(adapter_down_map, 'fsdp', axis=0, tiled=True)  28.9 us
    psum x1, waiting for transfers between devices, local(): down_shard = lax.psum(down_shard, ('dp', 'pair'))  26.3 us
    all_gather x1, blocking collectives, local(): lax.all_gather(values_gradient, 'fsdp', axis=0, tiled=True)  21.6 us
    all_gather x1, blocking collectives, local(): lax.all_gather(upward_product, 'fsdp', axis=0, tiled=True)  12 us
    psum x1, blocking collectives, local(): lax.psum(jnp.sum(down_shard * down_shard), 'fsdp')  11.2 us
  transfers between devices with their start and end apart: 4, of which 4 were waited for; matrix products, arithmetic and copies ran while one was open for 3% of the time, Pallas kernels for 0%

commit v1 on v0

v1 whole, which is shorter than its diff:
```python
import functools
import math

import jax
import jax.numpy as jnp
from jax import lax
from jax.experimental import pallas as pl
from jax.experimental.pallas import tpu as pltpu
from jax.sharding import PartitionSpec as P

norm_eps = 1e-05
adapter_scale = 2.0
MESH = pl.DeviceIdType.MESH
f32, bf16 = jnp.float32, jnp.bfloat16


def dot_nt(a, b):
    return lax.dot_general(a, b, (((1,), (1,)), ((), ())), preferred_element_type=f32)


def dot_tn(a, b):
    return lax.dot_general(a, b, (((0,), (0,)), ((), ())), preferred_element_type=f32)


def kernel(
    n, dp, pair,
    h, gain, w, dt, u, v,
    gh, gd, gu,
    vg, nm, cols, recv, dg, rd_send, rd_recv, rz_send, rz_recv, gd_all,
    pu_send, pu_recv, pz, gu_all, sq,
    v_send, v_sem, c_send, c_sem, da_send, da_sem, db_send, db_sem,
    rd_ssem, rd_rsem, rz_ssem, rz_rsem, gd_ssem, gd_rsem,
    pu_ssem, pu_rsem, pz_ssem, pz_rsem, gu_ssem, gu_rsem, sq_ssem, sq_rsem,
):
    m = dp * pair
    z = lax.axis_index("fsdp")
    p = lax.axis_index("dp") * pair + lax.axis_index("pair")
    tokens, width = h.shape
    features = w.shape[0]
    rank, r = u.shape[0], dt.shape[1]
    tile = min(512, features)

    def at_z(o):
        return {"fsdp": o}

    def at_p(q):
        return {"dp": lax.div(q, pair), "pair": lax.rem(q, pair)}

    def zpeer(d):
        return lax.rem(z + d, n)

    def ppeer(d):
        return lax.rem(p + d, m)

    def remote(src, dst, ssem, rsem, dev):
        return pltpu.make_async_remote_copy(
            src_ref=src, dst_ref=dst, send_sem=ssem, recv_sem=rsem,
            device_id=dev, device_id_type=MESH,
        )

    def each(count, body):
        if count <= 4:
            for d in range(1, count):
                body(d)
        else:
            pl.loop(1, count)(body)

    barrier = pltpu.get_barrier_semaphore()
    each(n, lambda d: pl.semaphore_signal(barrier, inc=1, device_id=at_z(zpeer(d)), device_id_type=MESH))
    each(m, lambda d: pl.semaphore_signal(barrier, inc=1, device_id=at_p(ppeer(d)), device_id_type=MESH))
    pl.semaphore_wait(barrier, n - 1 + m - 1)

    def v_right(src, o, k):
        return remote(src, vg.at[o], v_send.at[0, k], v_sem.at[o], at_z(jnp.minimum(z + 1, n - 1)))

    def v_left(src, o, k):
        return remote(src, vg.at[o], v_send.at[1, k], v_sem.at[o], at_z(jnp.maximum(z - 1, 0)))

    @pl.when(z < n - 1)
    def _():
        v_right(v, z, 0).start()

    @pl.when(z > 0)
    def _():
        v_left(v, z, 0).start()

    def da(d):
        return remote(dt.at[p], dg.at[p, z], da_send.at[d], da_sem.at[z], at_z(zpeer(d)))

    each(n, lambda d: da(d).start())
    dg[p, z] = dt[p]

    def upward_of(block):
        return (adapter_scale * dot_nt(block, u[...])).astype(bf16)

    def tiles(body, init, extent=width):
        def step(i, carry):
            return body(pl.ds(pl.multiple_of(i * tile, tile), tile), i, carry)
        return lax.fori_loop(0, extent // tile, step, init)

    def square(at, i, carry):
        x = h[:, at].astype(f32)
        return carry + jnp.sum(x * x, axis=1, keepdims=True)

    mean = tiles(square, jnp.zeros((tokens, 1), f32)) / width
    inv = lax.rsqrt(mean + norm_eps)
    up_own = upward_of(v[...])
    per = features // tile

    def down_part(at, i, carry):
        x = (h[:, at].astype(f32) * inv * gain[:, at]).astype(bf16)
        nm[:, at] = x
        part = dot_tn(up_own, x).astype(bf16)
        o = lax.div(i, per)
        inner = pl.ds(pl.multiple_of(lax.rem(i, per) * tile, tile), tile)
        for q in range(m):
            rd_send[q, o, :, inner] = part[q * r:(q + 1) * r]
        return carry

    tiles(down_part, 0)

    def rd(d):
        q = ppeer(d)
        return remote(rd_send.at[q], rd_recv.at[p], rd_ssem.at[d], rd_rsem.at[p], at_p(q))

    each(m, lambda d: rd(d).start())

    def columns(block, up, out):
        def step(at, i, carry):
            low = jnp.concatenate([dt[q, :, at] for q in range(m)], axis=0)
            acc = dot_nt(block, w[at, :]) + jnp.dot(up, low, preferred_element_type=f32)
            out[:, at] = acc.astype(bf16)
            return carry
        tiles(step, 0, features)

    def c_copy(o):
        return remote(cols.at[o], recv.at[z], c_send.at[o], c_sem.at[z], at_z(o))

    def c_wait(o):
        remote(cols.at[o], recv.at[o], c_send.at[o], c_sem.at[o], at_z(o)).wait_recv()

    def serve(o):
        block = vg[o]
        columns(block, upward_of(block), cols.at[o])
        c_copy(o).start()

    def v_step(k):
        left, right = z - 1 - k, z + 1 + k

        @pl.when(left >= 0)
        def _():
            v_right(vg.at[left], left, k + 1).wait_recv()

            @pl.when(z < n - 1)
            def _():
                v_right(vg.at[left], left, k + 1).start()

        @pl.when(right < n)
        def _():
            v_left(vg.at[right], right, k + 1).wait_recv()

            @pl.when(z > 0)
            def _():
                v_left(vg.at[right], right, k + 1).start()

        @pl.when(left >= 0)
        def _():
            serve(left)

        @pl.when(right < n)
        def _():
            serve(right)

    v_step(0)

    def da_wait(d):
        o = zpeer(d)
        remote(dt.at[p], dg.at[p, o], da_send.at[d], da_sem.at[o], at_z(o)).wait_recv()

    each(n, da_wait)

    def db(d):
        return remote(dg.at[p], dg.at[p], db_send.at[d], db_sem.at[p], at_p(ppeer(d)))

    each(m, lambda d: db(d).start())

    if n > 2:
        pl.loop(1, n - 1)(v_step)

    columns(v[...], up_own, recv.at[z])

    def rd_wait(d):
        q = ppeer(d)
        remote(rd_send.at[q], rd_recv.at[q], rd_ssem.at[d], rd_rsem.at[q], at_p(q)).wait_recv()

    each(m, rd_wait)

    def rz(d):
        o = zpeer(d)
        return remote(rz_send.at[o], rz_recv.at[z], rz_ssem.at[d], rz_rsem.at[z], at_z(o))

    def reduce_plane(d):
        o = zpeer(d)
        total = rd_send[p, o].astype(f32)
        for e in range(1, m):
            total = total + rd_recv[ppeer(e), o].astype(f32)
        rz_send[o] = total.astype(bf16)
        return total

    def reduce_and_send(d):
        reduce_plane(d)
        rz(d).start()

    each(n, reduce_and_send)
    gd_all[p] = reduce_plane(0)

    def db_wait(d):
        q = ppeer(d)
        remote(dg.at[q], dg.at[q], db_send.at[d], db_sem.at[q], at_p(q)).wait_recv()

    each(m, db_wait)

    def latent_part(at, i, carry):
        o = lax.div(i, per)
        inner = pl.ds(pl.multiple_of(lax.rem(i, per) * tile, tile), tile)
        low = jnp.concatenate([dg[q, o, :, inner] for q in range(m)], axis=0)
        return carry + dot_nt(nm[:, at], low)

    latent = tiles(latent_part, jnp.zeros((tokens, rank), f32)).astype(bf16)
    up_part = adapter_scale * dot_tn(latent, v[...])
    for q in range(m):
        pu_send[q] = up_part[q * r:(q + 1) * r]

    def pu(d):
        q = ppeer(d)
        return remote(pu_send.at[q], pu_recv.at[p], pu_ssem.at[d], pu_rsem.at[p], at_p(q))

    def pu_wait(d):
        q = ppeer(d)
        remote(pu_send.at[q], pu_recv.at[q], pu_ssem.at[d], pu_rsem.at[q], at_p(q)).wait_recv()

    each(m, lambda d: pu(d).start())
    each(m, pu_wait)
    total = pu_send[p]
    for e in range(1, m):
        total = total + pu_recv[ppeer(e)]
    pz[z] = total

    def pz_copy(d):
        return remote(pz.at[z], pz.at[z], pz_ssem.at[d], pz_rsem.at[z], at_z(zpeer(d)))

    def pz_wait(d):
        o = zpeer(d)
        remote(pz.at[o], pz.at[o], pz_ssem.at[d], pz_rsem.at[o], at_z(o)).wait_recv()

    each(n, lambda d: pz_copy(d).start())

    def rz_wait(d):
        o = zpeer(d)
        remote(rz_send.at[o], rz_recv.at[o], rz_ssem.at[d], rz_rsem.at[o], at_z(o)).wait_recv()
        gd_all[p] = gd_all[p] + rz_recv[o].astype(f32)

    each(n, rz_wait)

    def gd_copy(d):
        return remote(gd_all.at[p], gd_all.at[p], gd_ssem.at[d], gd_rsem.at[p], at_p(ppeer(d)))

    def gd_wait(d):
        q = ppeer(d)
        remote(gd_all.at[q], gd_all.at[q], gd_ssem.at[d], gd_rsem.at[q], at_p(q)).wait_recv()

    each(m, lambda d: gd_copy(d).start())
    each(n, pz_wait)
    total = pz[0]
    for o in range(1, n):
        total = total + pz[o]
    gu_all[p] = total

    def gu_copy(d):
        return remote(gu_all.at[p], gu_all.at[p], gu_ssem.at[d], gu_rsem.at[p], at_p(ppeer(d)))

    def gu_wait(d):
        q = ppeer(d)
        remote(gu_all.at[q], gu_all.at[q], gu_ssem.at[d], gu_rsem.at[q], at_p(q)).wait_recv()

    each(m, lambda d: gu_copy(d).start())
    each(m, gd_wait)

    def sum_squares(ref):
        out = jnp.zeros((1, 1), f32)
        for q in range(m):
            x = ref[q]
            x = jnp.sum(x * x, axis=0, keepdims=True)
            out = out + jnp.sum(x, axis=1, keepdims=True)
        return out

    sq[z] = jnp.broadcast_to(sum_squares(gd_all), sq.shape[1:])

    def sq_copy(d):
        return remote(sq.at[z], sq.at[z], sq_ssem.at[d], sq_rsem.at[z], at_z(zpeer(d)))

    def sq_wait(d):
        o = zpeer(d)
        remote(sq.at[o], sq.at[o], sq_ssem.at[d], sq_rsem.at[o], at_z(o)).wait_recv()

    each(n, lambda d: sq_copy(d).start())
    each(m, gu_wait)
    up_squares = sum_squares(gu_all)

    def inner_sum(o, carry):
        def step(at, i, carry):
            whole = pl.ds(pl.multiple_of(o * features + i * tile, tile), tile)
            scaled = recv[o, :, at].astype(f32) * gain[:, whole]
            return carry + jnp.sum(scaled * h[:, whole].astype(f32), axis=1, keepdims=True)
        return tiles(step, carry, features)

    dots = inner_sum(z, jnp.zeros((tokens, 1), f32))

    def arrive(d, dots):
        o = zpeer(d)
        c_wait(o)
        return inner_sum(o, dots)

    dots = lax.fori_loop(1, n, arrive, dots)
    coef = inv * inv * inv / width * dots

    def finish(at, i, carry):
        o = lax.div(i, per)
        inner = pl.ds(pl.multiple_of(lax.rem(i, per) * tile, tile), tile)
        scaled = recv[o, :, inner].astype(f32) * gain[:, at]
        gh[:, at] = (inv * scaled - h[:, at].astype(f32) * coef).astype(bf16)
        return carry

    tiles(finish, 0)

    each(n, sq_wait)
    total = sq[0][:1, :1]
    for o in range(1, n):
        total = total + sq[o][:1, :1]
    total = total + up_squares
    factor = jnp.minimum(1.0, 0.5 * math.sqrt(width * rank) / jnp.sqrt(total))
    for q in range(m):
        gd[q] = factor * gd_all[q]
        gu[q] = factor * gu_all[q]

    @pl.when(z < n - 1)
    def _():
        v_right(v, z, 0).wait_send()

    @pl.when(z > 0)
    def _():
        v_left(v, z, 0).wait_send()

    @pl.loop(0, n - 1)
    def _(k):
        @pl.when((z - 1 - k >= 0) & (z < n - 1))
        def _():
            v_right(v, z, k + 1).wait_send()

        @pl.when((z + 1 + k < n) & (z > 0))
        def _():
            v_left(v, z, k + 1).wait_send()

    def z_sent(d):
        for copy in (da(d), rz(d), pz_copy(d), sq_copy(d), c_copy(zpeer(d))):
            copy.wait_send()

    def p_sent(d):
        for copy in (rd(d), db(d), pu(d), gd_copy(d), gu_copy(d)):
            copy.wait_send()

    each(n, z_sent)
    each(m, p_sent)


def local(n, dp, pair, h, gain, w, d, u, v):
    m = dp * pair
    tokens, width = h.shape
    features, values = w.shape
    rank = u.shape[0]
    r = rank // m
    dt = d.T.reshape(m, r, features)
    vmem = pl.BlockSpec(memory_space=pltpu.VMEM)
    dma = pltpu.SemaphoreType.DMA
    z1, p1 = dma((n,)), dma((m,))
    gh, gd, gu = pl.pallas_call(
        functools.partial(kernel, n, dp, pair),
        out_shape=(
            jax.ShapeDtypeStruct((tokens, width), bf16),
            jax.ShapeDtypeStruct((m, r, features), f32),
            jax.ShapeDtypeStruct((m, r, values), f32),
        ),
        in_specs=[vmem] * 6,
        out_specs=(vmem,) * 3,
        scratch_shapes=[
            pltpu.VMEM((n, tokens, values), bf16),
            pltpu.VMEM((tokens, width), bf16),
            pltpu.VMEM((n, tokens, features), bf16),
            pltpu.VMEM((n, tokens, features), bf16),
            pltpu.VMEM((m, n, r, features), bf16),
            pltpu.VMEM((m, n, r, features), bf16),
            pltpu.VMEM((m, n, r, features), bf16),
            pltpu.VMEM((n, r, features), bf16),
            pltpu.VMEM((n, r, features), bf16),
            pltpu.VMEM((m, r, features), f32),
            pltpu.VMEM((m, r, values), f32),
            pltpu.VMEM((m, r, values), f32),
            pltpu.VMEM((n, r, values), f32),
            pltpu.VMEM((m, r, values), f32),
            pltpu.VMEM((n, 8, 128), f32),
            dma((2, n)), z1, z1, z1, z1, z1, p1, p1,
            p1, p1, z1, z1, p1, p1,
            p1, p1, z1, z1, p1, p1, z1, z1,
        ],
        compiler_params=pltpu.CompilerParams(
            collective_id=0, has_side_effects=True, vmem_limit_bytes=56 * 1024 * 1024
        ),
        name="fused",
    )(h, gain.reshape(1, width), w, dt, u, v)
    return gh, gd.reshape(rank, features).T, gu.reshape(rank, values)


def solution(mesh):
    shape = mesh.shape
    tokens = P(("groups", "fsdp", "dp", "pair"), None)
    return jax.shard_map(
        functools.partial(local, shape["fsdp"], shape["dp"], shape["pair"]),
        mesh=mesh,
        in_specs=(
            tokens, P(), P("fsdp", None), P(("groups", "fsdp"), None), P("groups", None), tokens,
        ),
        out_specs=(tokens, P(("groups", "fsdp"), None), P("groups", None)),
        check_vma=False,
    )
```

time: 323 us -> 94.1 us (0.29)
  waiting for transfers between devices: 190 us -> 0 us
  blocking collectives: 91.3 us -> 0 us
  Pallas kernels: 0 us -> 88.4 us
  between operations: 15.2 us -> 0.66 us
  other arithmetic: 13.9 us -> 0 us
  matrix products: 9.43 us -> 0 us
    psum x2 -> x0, waiting for transfers between devices: 118 us -> none  [the longest x1 92 us: local(): up_full = lax.psum(up_portion, ('fsdp', 'dp', 'pair'))]
    pallas_call x0 -> x1, Pallas kernels: none -> 88.4 us  [local(): pl.pallas_call(functools.partial(kernel, n, dp, pair), out_shape=(jax.Sha...]
    all_to_all x1 -> x0, blocking collectives: 46.4 us -> none  [local(): lax.all_to_all(columns.astype(jnp.bfloat16), 'fsdp', split_axis=0, concat...]
    reduce_scatter x1 -> x0, waiting for transfers between devices: 42.3 us -> none  [local(): lax.psum_scatter(contract_leading(window, upward_product), 'fsdp', scatte...]
    all_gather x2 -> x0, blocking collectives: 33.6 us -> none  [the longest x1 21.6 us: local(): lax.all_gather(values_gradient, 'fsdp', axis=0, tiled=True)]
    all_gather x1 -> x0, waiting for transfers between devices: 28.9 us -> none  [local(): lax.all_gather(adapter_down_map, 'fsdp', axis=0, tiled=True)]
    psum x1 -> x0, blocking collectives: 11.2 us -> none  [local(): lax.psum(jnp.sum(down_shard * down_shard), 'fsdp')]
    dot_general x5 -> x0, matrix products: 9.43 us -> none  [the longest x2 5.69 us: contract_leading(): lax.dot_general(left, right, (((0,), (0,)), ((), ())), preferred_element_...]
  transfers between devices with their start and end apart: 4 -> 0, of which waited for: 4 -> 0; matrix products, arithmetic and copies ran while one was open for 3% -> 0% of each run, Pallas kernels for 0% -> 0%
where the time goes in v1:
time: 94.1 us; the launch traced here: 93.7 us
  Pallas kernels  88.4 us (94%)
  local copies, waits for them, and re-layouts  4.64 us (5%)
    pallas_call x1, Pallas kernels, local(): pl.pallas_call(functools.partial(kernel, n, dp, pair), out_shape=(jax.Sha...  88.4 us
    unnamed x7, local copies, waits for them, and re-layouts  4.64 us

profile of v1, /device:TPU:0, one launch (start us, length us, event | category | flops | bytes accessed | tf_op | source)
XLA Modules:
  0.0 93.7 jit_solution(14615764581368691413)
XLA Ops:
  0.6 88.4 %fused.1 = (bf16[128,8192]{1,0:T(8,128)(2,1)}, f32[4,16,2048]{2,1,0:T(8,128)}, f32[4,16,768]{2,1,0:T(8,128)}) custom-call(bf16[128,8192]{1,0:T(8,128)(2,1)} %h.1, f32[1,8192]{1,0:T(1,128)} %bitcast.11, bf16[2048,768]{1,0:T(8,128)(2,1)} %w.1, bf16[4,16,2048]{2,1,0:T(8,128)(2,1)} %bitcast.9, bf16[64,768]{1,0:T(8,128)(2,1)} %u.1, bf16[128,768]{1,0:T(8,128)(2,1)} %v.1), custom_call_target="tpu_custom_call" | custom-call | tf_op jit(solution)/shard_map/fused/pallas_call | solution.py:386
  89.0 0.0 copy-start
  89.1 0.0 copy-start.1
  89.1 3.2 %copy.12 = bf16[128,8192]{1,0:T(8,128)(2,1)} copy(bf16[128,8192]{1,0:T(8,128)(2,1)} %get-tuple-element.12) | data formatting | bytes 4194304
  92.2 0.0 copy-done
  92.2 0.8 copy.13
  93.0 0.0 copy-done.1
  93.0 0.7 copy.14
Async XLA Ops:
  89.0 3.2 %copy-start = (f32[4,16,2048]{2,1,0:T(8,128)S(1)}, f32[4,16,2048]{2,1,0:T(8,128)}, u32[]{:S(2)}) copy-start(f32[4,16,2048]{2,1,0:T(8,128)} %get-tuple-element.7) | copy-start | bytes 1572868
  89.1 4.0 %copy-start.1 = (f32[4,16,768]{2,1,0:T(8,128)S(1)}, f32[4,16,768]{2,1,0:T(8,128)}, u32[]{:S(2)}) copy-start(f32[4,16,768]{2,1,0:T(8,128)} %get-tuple-element.8) | copy-start | bytes 589828

commit v2 on v1

--- a/solution.py
+++ b/solution.py
@@ -23,12 +23,13 @@
 
 
 def kernel(
-    n, dp, pair,
+    n, groups, dp, pair, head,
     h, gain, w, dt, u, v,
     gh, gd, gu,
-    vg, nm, cols, recv, dg, rd_send, rd_recv, rz_send, rz_recv, gd_all,
+    vg, nm, ws, cols, cols_head, recv, recv_head, dg, rd_send, rd_recv, rz_send, rz_recv, gd_all,
     pu_send, pu_recv, pz, gu_all, sq,
-    v_send, v_sem, c_send, c_sem, da_send, da_sem, db_send, db_sem,
+    v_send, v_sem, w_send, w_sem, s_send, s_sem, f_send, f_sem,
+    c_send, c_sem, h_send, h_sem, da_send, da_sem, db_send, db_sem,
     rd_ssem, rd_rsem, rz_ssem, rz_rsem, gd_ssem, gd_rsem,
     pu_ssem, pu_rsem, pz_ssem, pz_rsem, gu_ssem, gu_rsem, sq_ssem, sq_rsem,
 ):
@@ -37,6 +38,10 @@
     p = lax.axis_index("dp") * pair + lax.axis_index("pair")
     tokens, width = h.shape
     features = w.shape[0]
+    body = features - head
+    chips, rows = ws.shape[2], ws.shape[3]
+    g, x, c = lax.axis_index("groups"), lax.axis_index("dp"), lax.axis_index("pair")
+    chip = g * dp + x
     rank, r = u.shape[0], dt.shape[1]
     tile = min(512, features)
 
@@ -45,6 +50,16 @@
 
     def at_p(q):
         return {"dp": lax.div(q, pair), "pair": lax.rem(q, pair)}
+
+    def at_chip(d):
+        q = lax.rem(chip + d, chips)
+        return {"groups": lax.div(q, dp), "dp": lax.rem(q, dp)}
+
+    def at_core(d):
+        return {"pair": lax.rem(c + d, pair)}
+
+    def far(o):
+        return (o < n // 2) != (z < n // 2)
 
     def zpeer(d):
         return lax.rem(z + d, n)
@@ -68,26 +83,48 @@
     barrier = pltpu.get_barrier_semaphore()
     each(n, lambda d: pl.semaphore_signal(barrier, inc=1, device_id=at_z(zpeer(d)), device_id_type=MESH))
     each(m, lambda d: pl.semaphore_signal(barrier, inc=1, device_id=at_p(ppeer(d)), device_id_type=MESH))
-    pl.semaphore_wait(barrier, n - 1 + m - 1)
-
-    def v_right(src, o, k):
-        return remote(src, vg.at[o], v_send.at[0, k], v_sem.at[o], at_z(jnp.minimum(z + 1, n - 1)))
-
-    def v_left(src, o, k):
-        return remote(src, vg.at[o], v_send.at[1, k], v_sem.at[o], at_z(jnp.maximum(z - 1, 0)))
+    others = 0
+    if head:
+        others = (groups - 1) * dp
+        for d in range(1, groups):
+            for e in range(dp):
+                pl.semaphore_signal(
+                    barrier, inc=1, device_id_type=MESH,
+                    device_id={"groups": lax.rem(g + d, groups), "dp": lax.rem(x + e, dp)},
+                )
+    pl.semaphore_wait(barrier, n - 1 + m - 1 + others)
+
+    own_w = w.at[pl.ds(pl.multiple_of((c * chips + chip) * rows, rows), rows)]
+
+    def relay(kind, side, k, o, own=False):
+        device = at_z(jnp.minimum(z + 1, n - 1) if side == 0 else jnp.maximum(z - 1, 0))
+        if kind == "v":
+            dst, ssem, rsem, mine = vg.at[o], v_send, v_sem, v
+        elif kind == "d":
+            dst, ssem, rsem, mine = dg.at[p, o], da_send, da_sem, dt.at[p]
+        else:
+            dst, ssem, rsem, mine = ws.at[o, c, chip], w_send, w_sem, own_w
+        return remote(mine if own else dst, dst, ssem.at[side, k], rsem.at[o], device)
+
+    kinds = ("v", "d", "w") if head else ("v", "d")
 
     @pl.when(z < n - 1)
     def _():
-        v_right(v, z, 0).start()
+        relay("v", 0, 0, z, True).start()
 
     @pl.when(z > 0)
     def _():
-        v_left(v, z, 0).start()
-
-    def da(d):
-        return remote(dt.at[p], dg.at[p, z], da_send.at[d], da_sem.at[z], at_z(zpeer(d)))
-
-    each(n, lambda d: da(d).start())
+        relay("v", 1, 0, z, True).start()
+
+    for kind in kinds[1:]:
+        @pl.when(z < n - 1)
+        def _():
+            relay(kind, 0, 0, z, True).start()
+
+        @pl.when(z > 0)
+        def _():
+            relay(kind, 1, 0, z, True).start()
+
     dg[p, z] = dt[p]
 
     def upward_of(block):
@@ -125,69 +162,102 @@
 
     each(m, lambda d: rd(d).start())
 
-    def columns(block, up, out):
-        def step(at, i, carry):
+    def columns(block, up, out, start, extent):
+        width_of = min(tile, extent)
+
+        def step(i, carry):
+            to = pl.ds(pl.multiple_of(i * width_of, width_of), width_of)
+            at = pl.ds(pl.multiple_of(start + i * width_of, width_of), width_of)
             low = jnp.concatenate([dt[q, :, at] for q in range(m)], axis=0)
             acc = dot_nt(block, w[at, :]) + jnp.dot(up, low, preferred_element_type=f32)
-            out[:, at] = acc.astype(bf16)
+            out[:, to] = acc.astype(bf16)
             return carry
-        tiles(step, 0, features)
-
-    def c_copy(o):
-        return remote(cols.at[o], recv.at[z], c_send.at[o], c_sem.at[z], at_z(o))
-
-    def c_wait(o):
-        remote(cols.at[o], recv.at[o], c_send.at[o], c_sem.at[o], at_z(o)).wait_recv()
+        lax.fori_loop(0, extent // width_of, step, 0)
+
+    def c_copy(o, slot):
+        return remote(cols.at[o], recv.at[slot], c_send.at[o], c_sem.at[slot], at_z(o))
+
+    def h_copy(o, slot):
+        return remote(
+            cols_head.at[o], recv_head.at[slot], h_send.at[o], h_sem.at[slot], at_z(o)
+        )
 
     def serve(o):
         block = vg[o]
-        columns(block, upward_of(block), cols.at[o])
-        c_copy(o).start()
+        up = upward_of(block)
+        columns(block, up, cols.at[o], head, body)
+        c_copy(o, z).start()
+        if head:
+            @pl.when(jnp.logical_not(far(o)))
+            def _():
+                columns(block, up, cols_head.at[o], 0, head)
+                h_copy(o, z).start()
+
+    def share(o, d):
+        return remote(
+            ws.at[o, c, chip], ws.at[o, c, chip], s_send.at[o, d], s_sem.at[o, chip], at_chip(d)
+        )
+
+    def share_wait(o, d):
+        q = lax.rem(chip + d, chips)
+        remote(
+            ws.at[o, c, q], ws.at[o, c, q], s_send.at[o, d], s_sem.at[o, q], at_chip(d)
+        ).wait_recv()
+
+    def pass_on(o, d, core):
+        return remote(
+            ws.at[o, core], ws.at[o, core], f_send.at[o, d], f_sem.at[o, core], at_core(d)
+        )
+
+    def each_far(fn):
+        @pl.loop(0, n)
+        def _(o):
+            @pl.when(far(o))
+            def _():
+                fn(o)
+
+    def take(kind, side, k, o):
+        relay(kind, side, k, o).wait_recv()
+
+        @pl.when((z < n - 1) if side == 0 else (z > 0))
+        def _():
+            relay(kind, side, k, o).start()
 
     def v_step(k):
         left, right = z - 1 - k, z + 1 + k
 
-        @pl.when(left >= 0)
-        def _():
-            v_right(vg.at[left], left, k + 1).wait_recv()
-
-            @pl.when(z < n - 1)
+        def both(fn):
+            @pl.when(left >= 0)
             def _():
-                v_right(vg.at[left], left, k + 1).start()
-
-        @pl.when(right < n)
-        def _():
-            v_left(vg.at[right], right, k + 1).wait_recv()
-
-            @pl.when(z > 0)
+                fn(0, left)
+
+            @pl.when(right < n)
             def _():
-                v_left(vg.at[right], right, k + 1).start()
-
-        @pl.when(left >= 0)
-        def _():
-            serve(left)
-
-        @pl.when(right < n)
-        def _():
-            serve(right)
-
-    v_step(0)
-
-    def da_wait(d):
-        o = zpeer(d)
-        remote(dt.at[p], dg.at[p, o], da_send.at[d], da_sem.at[o], at_z(o)).wait_recv()
-
-    each(n, da_wait)
+                fn(1, right)
+
+        both(lambda side, o: take("v", side, k + 1, o))
+        both(lambda side, o: serve(o))
+
+        def weights(side, o):
+            for kind in kinds[1:]:
+                take(kind, side, k + 1, o)
+            if head:
+                @pl.when(far(o))
+                def _():
+                    for d in range(1, chips):
+                        share(o, d).start()
+
+        both(weights)
+
+    pl.loop(0, n - 1)(v_step)
 
     def db(d):
         return remote(dg.at[p], dg.at[p], db_send.at[d], db_sem.at[p], at_p(ppeer(d)))
 
     each(m, lambda d: db(d).start())
-
-    if n > 2:
-        pl.loop(1, n - 1)(v_step)
-
-    columns(v[...], up_own, recv.at[z])
+    columns(v[...], up_own, recv.at[z], head, body)
+    if head:
+        columns(v[...], up_own, recv_head.at[z], 0, head)
 
     def rd_wait(d):
         q = ppeer(d)
@@ -214,6 +284,15 @@
     each(n, reduce_and_send)
     gd_all[p] = reduce_plane(0)
 
+    if head:
+        def gather(o):
+            for d in range(1, chips):
+                share_wait(o, d)
+            for d in range(1, pair):
+                pass_on(o, d, c).start()
+
+        each_far(gather)
+
     def db_wait(d):
         q = ppeer(d)
         remote(dg.at[q], dg.at[q], db_send.at[d], db_sem.at[q], at_p(q)).wait_recv()
@@ -244,7 +323,7 @@
     total = pu_send[p]
     for e in range(1, m):
         total = total + pu_recv[ppeer(e)]
-    pz[z] = total
+    pz[z] = total.astype(bf16)
 
     def pz_copy(d):
         return remote(pz.at[z], pz.at[z], pz_ssem.at[d], pz_rsem.at[z], at_z(zpeer(d)))
@@ -271,9 +350,9 @@
 
     each(m, lambda d: gd_copy(d).start())
     each(n, pz_wait)
-    total = pz[0]
+    total = pz[0].astype(f32)
     for o in range(1, n):
-        total = total + pz[o]
+        total = total + pz[o].astype(f32)
     gu_all[p] = total
 
     def gu_copy(d):
@@ -307,31 +386,57 @@
     each(m, gu_wait)
     up_squares = sum_squares(gu_all)
 
+    if head:
+        def own_head(o):
+            for d in range(1, pair):
+                pass_on(o, d, lax.rem(c + d, pair)).wait_recv()
+            for e in range(pair):
+                size = chips * rows
+                at = slice(e * size, (e + 1) * size)
+                low = jnp.concatenate([dg[q, o, :, at] for q in range(m)], axis=0)
+                acc = dot_nt(v[...], ws[o, e].reshape(size, v.shape[1]))
+                acc = acc + jnp.dot(up_own, low, preferred_element_type=f32)
+                recv_head[o, :, at] = acc.astype(bf16)
+
+        each_far(own_head)
+
+    def sweep(o, source, start, extent, carry, body_of):
+        size = min(tile, extent)
+
+        def step(i, carry):
+            at = pl.ds(pl.multiple_of(o * features + start + i * size, size), size)
+            scaled = source[o, :, pl.ds(pl.multiple_of(i * size, size), size)].astype(f32) * gain[:, at]
+            return body_of(scaled, at, carry)
+        return lax.fori_loop(0, extent // size, step, carry)
+
+    def both_parts(o, carry, body_of):
+        if head:
+            carry = sweep(o, recv_head, 0, head, carry, body_of)
+        return sweep(o, recv, head, body, carry, body_of)
+
     def inner_sum(o, carry):
-        def step(at, i, carry):
-            whole = pl.ds(pl.multiple_of(o * features + i * tile, tile), tile)
-            scaled = recv[o, :, at].astype(f32) * gain[:, whole]
-            return carry + jnp.sum(scaled * h[:, whole].astype(f32), axis=1, keepdims=True)
-        return tiles(step, carry, features)
+        return both_parts(o, carry, lambda scaled, at, total: total + jnp.sum(
+            scaled * h[:, at].astype(f32), axis=1, keepdims=True))
 
     dots = inner_sum(z, jnp.zeros((tokens, 1), f32))
 
     def arrive(d, dots):
         o = zpeer(d)
-        c_wait(o)
+        c_copy(o, o).wait_recv()
+        if head:
+            @pl.when(jnp.logical_not(far(o)))
+            def _():
+                h_copy(o, o).wait_recv()
         return inner_sum(o, dots)
 
     dots = lax.fori_loop(1, n, arrive, dots)
     coef = inv * inv * inv / width * dots
 
-    def finish(at, i, carry):
-        o = lax.div(i, per)
-        inner = pl.ds(pl.multiple_of(lax.rem(i, per) * tile, tile), tile)
-        scaled = recv[o, :, inner].astype(f32) * gain[:, at]
+    def finish(scaled, at, carry):
         gh[:, at] = (inv * scaled - h[:, at].astype(f32) * coef).astype(bf16)
         return carry
 
-    tiles(finish, 0)
+    lax.fori_loop(0, n, lambda o, carry: both_parts(o, carry, finish), 0)
 
     each(n, sq_wait)
     total = sq[0][:1, :1]
@@ -343,48 +448,70 @@
         gd[q] = factor * gd_all[q]
         gu[q] = factor * gu_all[q]
 
+    def sent(side, k, o):
+        for kind in kinds:
+            relay(kind, side, k, o).wait_send()
+
     @pl.when(z < n - 1)
     def _():
-        v_right(v, z, 0).wait_send()
+        sent(0, 0, z)
 
     @pl.when(z > 0)
     def _():
-        v_left(v, z, 0).wait_send()
+        sent(1, 0, z)
 
     @pl.loop(0, n - 1)
     def _(k):
         @pl.when((z - 1 - k >= 0) & (z < n - 1))
         def _():
-            v_right(v, z, k + 1).wait_send()
+            sent(0, k + 1, z)
 
         @pl.when((z + 1 + k < n) & (z > 0))
         def _():
-            v_left(v, z, k + 1).wait_send()
+            sent(1, k + 1, z)
 
     def z_sent(d):
-        for copy in (da(d), rz(d), pz_copy(d), sq_copy(d), c_copy(zpeer(d))):
+        o = zpeer(d)
+        for copy in (rz(d), pz_copy(d), sq_copy(d), c_copy(o, z)):
             copy.wait_send()
+        if head:
+            @pl.when(jnp.logical_not(far(o)))
+            def _():
+                h_copy(o, z).wait_send()
 
     def p_sent(d):
         for copy in (rd(d), db(d), pu(d), gd_copy(d), gu_copy(d)):
             copy.wait_send()
 
+    if head:
+        def far_sent(o):
+            for d in range(1, chips):
+                share(o, d).wait_send()
+            for d in range(1, pair):
+                pass_on(o, d, c).wait_send()
+
+        each_far(far_sent)
+
     each(n, z_sent)
     each(m, p_sent)
 
 
-def local(n, dp, pair, h, gain, w, d, u, v):
+def local(n, groups, dp, pair, h, gain, w, d, u, v):
     m = dp * pair
     tokens, width = h.shape
     features, values = w.shape
     rank = u.shape[0]
     r = rank // m
+    slices = groups * m
+    head = features // 2 if (features // 2) % (slices * 128) == 0 else 0
+    rows = max(head // slices, 16)
+    kept = max(head, 128)
     dt = d.T.reshape(m, r, features)
     vmem = pl.BlockSpec(memory_space=pltpu.VMEM)
     dma = pltpu.SemaphoreType.DMA
     z1, p1 = dma((n,)), dma((m,))
     gh, gd, gu = pl.pallas_call(
-        functools.partial(kernel, n, dp, pair),
+        functools.partial(kernel, n, groups, dp, pair, head),
         out_shape=(
             jax.ShapeDtypeStruct((tokens, width), bf16),
             jax.ShapeDtypeStruct((m, r, features), f32),
@@ -395,8 +522,11 @@
         scratch_shapes=[
             pltpu.VMEM((n, tokens, values), bf16),
             pltpu.VMEM((tokens, width), bf16),
-            pltpu.VMEM((n, tokens, features), bf16),
-            pltpu.VMEM((n, tokens, features), bf16),
+            pltpu.VMEM((n, pair, groups * dp, rows, values), bf16),
+            pltpu.VMEM((n, tokens, features - head), bf16),
+            pltpu.VMEM((n, tokens, kept), bf16),
+            pltpu.VMEM((n, tokens, features - head), bf16),
+            pltpu.VMEM((n, tokens, kept), bf16),
             pltpu.VMEM((m, n, r, features), bf16),
             pltpu.VMEM((m, n, r, features), bf16),
             pltpu.VMEM((m, n, r, features), bf16),
@@ -405,10 +535,12 @@
             pltpu.VMEM((m, r, features), f32),
             pltpu.VMEM((m, r, values), f32),
             pltpu.VMEM((m, r, values), f32),
-            pltpu.VMEM((n, r, values), f32),
+            pltpu.VMEM((n, r, values), bf16),
             pltpu.VMEM((m, r, values), f32),
             pltpu.VMEM((n, 8, 128), f32),
-            dma((2, n)), z1, z1, z1, z1, z1, p1, p1,
+            dma((2, n)), z1, dma((2, n)), z1,
+            dma((n, groups * dp)), dma((n, groups * dp)), dma((n, pair)), dma((n, pair)),
+            z1, z1, z1, z1, dma((2, n)), z1, p1, p1,
             p1, p1, z1, z1, p1, p1,
             p1, p1, z1, z1, p1, p1, z1, z1,
         ],
@@ -424,7 +556,7 @@
     shape = mesh.shape
     tokens = P(("groups", "fsdp", "dp", "pair"), None)
     return jax.shard_map(
-        functools.partial(local, shape["fsdp"], shape["dp"], shape["pair"]),
+        functools.partial(local, shape["fsdp"], shape["groups"], shape["dp"], shape["pair"]),
         mesh=mesh,
         in_specs=(
             tokens, P(), P("fsdp", None), P(("groups", "fsdp"), None), P("groups", None), tokens,

time: 94.1 us -> 111 us (1.18)
  Pallas kernels: 88.4 us -> 105 us
    pallas_call x1, Pallas kernels: 88.4 us -> 105 us  [local(): pl.pallas_call(functools.partial(kernel, n, groups, dp, pair, head), out_...]
where the time goes in v2:
time: 111 us
  Pallas kernels  105 us (95%)
  local copies, waits for them, and re-layouts  4.64 us (4%)
    pallas_call x1, Pallas kernels, local(): pl.pallas_call(functools.partial(kernel, n, groups, dp, pair, head), out_...  105 us
    unnamed x7, local copies, waits for them, and re-layouts  4.64 us

profile of v2, /device:TPU:0, one launch (start us, length us, event | category | flops | bytes accessed | tf_op | source)
XLA Modules:
  0.0 110.6 jit_solution(3229181382043321581)
XLA Ops:
  0.6 105.3 %fused.1 = (bf16[128,8192]{1,0:T(8,128)(2,1)}, f32[4,16,2048]{2,1,0:T(8,128)}, f32[4,16,768]{2,1,0:T(8,128)}) custom-call(bf16[128,8192]{1,0:T(8,128)(2,1)} %h.1, f32[1,8192]{1,0:T(1,128)} %bitcast.11, bf16[2048,768]{1,0:T(8,128)(2,1)} %w.1, bf16[4,16,2048]{2,1,0:T(8,128)(2,1)} %bitcast.9, bf16[64,768]{1,0:T(8,128)(2,1)} %u.1, bf16[128,768]{1,0:T(8,128)(2,1)} %v.1), custom_call_target="tpu_custom_call" | custom-call | tf_op jit(solution)/shard_map/fused/pallas_call | solution.py:513
  106.0 0.0 copy-start
  106.0 0.0 copy-start.1
  106.0 3.2 %copy.12 = bf16[128,8192]{1,0:T(8,128)(2,1)} copy(bf16[128,8192]{1,0:T(8,128)(2,1)} %get-tuple-element.12) | data formatting | bytes 4194304
  109.2 0.0 copy-done
  109.2 0.8 copy.13
  109.9 0.0 copy-done.1
  110.0 0.7 copy.14
Async XLA Ops:
  106.0 3.2 %copy-start = (f32[4,16,2048]{2,1,0:T(8,128)S(1)}, f32[4,16,2048]{2,1,0:T(8,128)}, u32[]{:S(2)}) copy-start(f32[4,16,2048]{2,1,0:T(8,128)} %get-tuple-element.7) | copy-start | bytes 1572868
  106.0 4.0 %copy-start.1 = (f32[4,16,768]{2,1,0:T(8,128)S(1)}, f32[4,16,768]{2,1,0:T(8,128)}, u32[]{:S(2)}) copy-start(f32[4,16,768]{2,1,0:T(8,128)} %get-tuple-element.8) | copy-start | bytes 589828

commit v3 on v2

--- a/solution.py
+++ b/solution.py
@@ -223,41 +223,41 @@
         def _():
             relay(kind, side, k, o).start()
 
-    def v_step(k):
+    def both(k, fn):
         left, right = z - 1 - k, z + 1 + k
 
-        def both(fn):
-            @pl.when(left >= 0)
-            def _():
-                fn(0, left)
-
-            @pl.when(right < n)
-            def _():
-                fn(1, right)
-
-        both(lambda side, o: take("v", side, k + 1, o))
-        both(lambda side, o: serve(o))
-
-        def weights(side, o):
-            for kind in kinds[1:]:
-                take(kind, side, k + 1, o)
-            if head:
+        @pl.when(left >= 0)
+        def _():
+            fn(0, left)
+
+        @pl.when(right < n)
+        def _():
+            fn(1, right)
+
+    def relay_step(k):
+        both(k, lambda side, o: take("v", side, k + 1, o))
+        both(k, lambda side, o: take("d", side, k + 1, o))
+        if head:
+            both(k, lambda side, o: take("w", side, k + 1, o))
+
+            def spread(side, o):
                 @pl.when(far(o))
                 def _():
                     for d in range(1, chips):
                         share(o, d).start()
 
-        both(weights)
-
-    pl.loop(0, n - 1)(v_step)
+            both(k, spread)
+
+    def serve_step(k):
+        both(k, lambda side, o: serve(o))
+
+    pl.loop(0, n - 1)(relay_step)
 
     def db(d):
         return remote(dg.at[p], dg.at[p], db_send.at[d], db_sem.at[p], at_p(ppeer(d)))
 
     each(m, lambda d: db(d).start())
-    columns(v[...], up_own, recv.at[z], head, body)
-    if head:
-        columns(v[...], up_own, recv_head.at[z], 0, head)
+    pl.loop(0, n - 1)(serve_step)
 
     def rd_wait(d):
         q = ppeer(d)
@@ -293,6 +293,10 @@
 
         each_far(gather)
 
+    columns(v[...], up_own, recv.at[z], head, body)
+    if head:
+        columns(v[...], up_own, recv_head.at[z], 0, head)
+
     def db_wait(d):
         q = ppeer(d)
         remote(dg.at[q], dg.at[q], db_send.at[d], db_sem.at[q], at_p(q)).wait_recv()
@@ -349,43 +353,6 @@
         remote(gd_all.at[q], gd_all.at[q], gd_ssem.at[d], gd_rsem.at[q], at_p(q)).wait_recv()
 
     each(m, lambda d: gd_copy(d).start())
-    each(n, pz_wait)
-    total = pz[0].astype(f32)
-    for o in range(1, n):
-        total = total + pz[o].astype(f32)
-    gu_all[p] = total
-
-    def gu_copy(d):
-        return remote(gu_all.at[p], gu_all.at[p], gu_ssem.at[d], gu_rsem.at[p], at_p(ppeer(d)))
-
-    def gu_wait(d):
-        q = ppeer(d)
-        remote(gu_all.at[q], gu_all.at[q], gu_ssem.at[d], gu_rsem.at[q], at_p(q)).wait_recv()
-
-    each(m, lambda d: gu_copy(d).start())
-    each(m, gd_wait)
-
-    def sum_squares(ref):
-        out = jnp.zeros((1, 1), f32)
-        for q in range(m):
-            x = ref[q]
-            x = jnp.sum(x * x, axis=0, keepdims=True)
-            out = out + jnp.sum(x, axis=1, keepdims=True)
-        return out
-
-    sq[z] = jnp.broadcast_to(sum_squares(gd_all), sq.shape[1:])
-
-    def sq_copy(d):
-        return remote(sq.at[z], sq.at[z], sq_ssem.at[d], sq_rsem.at[z], at_z(zpeer(d)))
-
-    def sq_wait(d):
-        o = zpeer(d)
-        remote(sq.at[o], sq.at[o], sq_ssem.at[d], sq_rsem.at[o], at_z(o)).wait_recv()
-
-    each(n, lambda d: sq_copy(d).start())
-    each(m, gu_wait)
-    up_squares = sum_squares(gu_all)
-
     if head:
         def own_head(o):
             for d in range(1, pair):
@@ -430,6 +397,42 @@
         return inner_sum(o, dots)
 
     dots = lax.fori_loop(1, n, arrive, dots)
+    each(m, gd_wait)
+
+    def sum_squares(ref):
+        out = jnp.zeros((1, 1), f32)
+        for q in range(m):
+            x = ref[q]
+            x = jnp.sum(x * x, axis=0, keepdims=True)
+            out = out + jnp.sum(x, axis=1, keepdims=True)
+        return out
+
+    sq[z] = jnp.broadcast_to(sum_squares(gd_all), sq.shape[1:])
+
+    def sq_copy(d):
+        return remote(sq.at[z], sq.at[z], sq_ssem.at[d], sq_rsem.at[z], at_z(zpeer(d)))
+
+    def sq_wait(d):
+        o = zpeer(d)
+        remote(sq.at[o], sq.at[o], sq_ssem.at[d], sq_rsem.at[o], at_z(o)).wait_recv()
+
+    each(n, lambda d: sq_copy(d).start())
+
+    each(n, pz_wait)
+    total = pz[0].astype(f32)
+    for o in range(1, n):
+        total = total + pz[o].astype(f32)
+    gu_all[p] = total
+
+    def gu_copy(d):
+        return remote(gu_all.at[p], gu_all.at[p], gu_ssem.at[d], gu_rsem.at[p], at_p(ppeer(d)))
+
+    def gu_wait(d):
+        q = ppeer(d)
+        remote(gu_all.at[q], gu_all.at[q], gu_ssem.at[d], gu_rsem.at[q], at_p(q)).wait_recv()
+
+    each(m, lambda d: gu_copy(d).start())
+
     coef = inv * inv * inv / width * dots
 
     def finish(scaled, at, carry):
@@ -437,6 +440,9 @@
         return carry
 
     lax.fori_loop(0, n, lambda o, carry: both_parts(o, carry, finish), 0)
+
+    each(m, gu_wait)
+    up_squares = sum_squares(gu_all)
 
     each(n, sq_wait)
     total = sq[0][:1, :1]
@@ -503,7 +509,7 @@
     rank = u.shape[0]
     r = rank // m
     slices = groups * m
-    head = features // 2 if (features // 2) % (slices * 128) == 0 else 0
+    head = features // 4 if (features // 4) % (slices * 64) == 0 else 0
     rows = max(head // slices, 16)
     kept = max(head, 128)
     dt = d.T.reshape(m, r, features)

time: 111 us -> 86.1 us (0.78)
  Pallas kernels: 105 us -> 80.6 us
    pallas_call x1, Pallas kernels: 105 us -> 80.6 us  [local(): pl.pallas_call(functools.partial(kernel, n, groups, dp, pair, head), out_...]
where the time goes in v3:
time: 86.1 us; the launch traced here: 85.9 us
  Pallas kernels  80.6 us (94%)
  local copies, waits for them, and re-layouts  4.64 us (5%)
    pallas_call x1, Pallas kernels, local(): pl.pallas_call(functools.partial(kernel, n, groups, dp, pair, head), out_...  80.6 us
    unnamed x7, local copies, waits for them, and re-layouts  4.64 us

profile of v3, /device:TPU:0, one launch (start us, length us, event | category | flops | bytes accessed | tf_op | source)
XLA Modules:
  0.0 85.9 jit_solution(14644126565730591457)
XLA Ops:
  0.6 80.6 %fused.1 = (bf16[128,8192]{1,0:T(8,128)(2,1)}, f32[4,16,2048]{2,1,0:T(8,128)}, f32[4,16,768]{2,1,0:T(8,128)}) custom-call(bf16[128,8192]{1,0:T(8,128)(2,1)} %h.1, f32[1,8192]{1,0:T(1,128)} %bitcast.11, bf16[2048,768]{1,0:T(8,128)(2,1)} %w.1, bf16[4,16,2048]{2,1,0:T(8,128)(2,1)} %bitcast.9, bf16[64,768]{1,0:T(8,128)(2,1)} %u.1, bf16[128,768]{1,0:T(8,128)(2,1)} %v.1), custom_call_target="tpu_custom_call" | custom-call | tf_op jit(solution)/shard_map/fused/pallas_call | solution.py:519
  81.3 0.0 copy-start
  81.3 0.0 copy-start.1
  81.3 3.2 %copy.12 = bf16[128,8192]{1,0:T(8,128)(2,1)} copy(bf16[128,8192]{1,0:T(8,128)(2,1)} %get-tuple-element.12) | data formatting | bytes 4194304
  84.5 0.0 copy-done
  84.5 0.8 copy.13
  85.3 0.0 copy-done.1
  85.3 0.7 copy.14
Async XLA Ops:
  81.3 3.2 %copy-start = (f32[4,16,2048]{2,1,0:T(8,128)S(1)}, f32[4,16,2048]{2,1,0:T(8,128)}, u32[]{:S(2)}) copy-start(f32[4,16,2048]{2,1,0:T(8,128)} %get-tuple-element.7) | copy-start | bytes 1572868
  81.3 4.0 %copy-start.1 = (f32[4,16,768]{2,1,0:T(8,128)S(1)}, f32[4,16,768]{2,1,0:T(8,128)}, u32[]{:S(2)}) copy-start(f32[4,16,768]{2,1,0:T(8,128)} %get-tuple-element.8) | copy-start | bytes 589828
